TPU v7x, 32 devices: a whole 2x2x4 slice. The times are simulated.
32 devices in a mesh: seq: 8 (over z, y), fsdp: 4 (over x, core).
Axes of the slice: x: 2, y: 2, z: 4, core: 2. Of those that a mesh axis runs over, the one named last changes fastest.
Arguments:
- inputs: float32 [8, 56, 28, 512], P('fsdp', 'seq'), may hold values from -6 to 6
- out_grad: float32 [8, 56, 28, 512], P('fsdp', 'seq'), may hold values from -6 to 6
- regions: int32 [56, 28], P('seq'), may hold values from 0 to 127, as said below
- rel_index: int32 [49, 49], replicated, may hold values from 0 to 168, as said below
- qkv_weight: float32 [512, 1536], P('fsdp'), may hold values from -0.25 to 0.25
- qkv_first: float32 [512, 1536], P('fsdp'), may hold values from -80 to 80
- qkv_second: float32 [512, 1536], P('fsdp'), may hold values from 12.544 to 50.176
- proj_weight: float32 [512, 512], P('fsdp'), may hold values from -0.75 to 0.75
- proj_first: float32 [512, 512], P('fsdp'), may hold values from -40 to 40
- proj_second: float32 [512, 512], P('fsdp'), may hold values from 3.136 to 12.544
- up_weight: float32 [512, 2048], P('fsdp'), may hold values from -0.25 to 0.25
- up_first: float32 [512, 2048], P('fsdp'), may hold values from -24 to 24
- up_second: float32 [512, 2048], P('fsdp'), may hold values from 1.12896 to 4.51584
- down_weight: float32 [2048, 512], P('fsdp'), may hold values from -0.125 to 0.125
- down_first: float32 [2048, 512], P('fsdp'), may hold values from -48 to 48
- down_second: float32 [2048, 512], P('fsdp'), may hold values from 5.0176 to 21.3248
- vectors: float32 [6144], replicated, may hold values from -0.6 to 1.4, as said below
- vectors_first: float32 [6144], replicated, may hold values from -64 to 64
- vectors_second: float32 [6144], replicated, may hold values from 2.5088 to 50.176
- bias_table: float32 [16, 169], replicated, may hold values from -5 to 5
- table_first: float32 [16, 169], replicated, may hold values from -80 to 80
- table_second: float32 [16, 169], replicated, may hold values from 12.544 to 50.176
Outputs:
- block_out: float32 [8, 56, 28, 512], P('fsdp', 'seq')
- input_grad: float32 [8, 56, 28, 512], P('fsdp', 'seq')
- new_qkv: float32 [512, 1536], P('fsdp')
- new_qkv_first: float32 [512, 1536], P('fsdp')
- new_qkv_second: float32 [512, 1536], P('fsdp')
- new_proj: float32 [512, 512], P('fsdp')
- new_proj_first: float32 [512, 512], P('fsdp')
- new_proj_second: float32 [512, 512], P('fsdp')
- new_up: float32 [512, 2048], P('fsdp')
- new_up_first: float32 [512, 2048], P('fsdp')
- new_up_second: float32 [512, 2048], P('fsdp')
- new_down: float32 [2048, 512], P('fsdp')
- new_down_first: float32 [2048, 512], P('fsdp')
- new_down_second: float32 [2048, 512], P('fsdp')
- new_vectors: float32 [6144], replicated
- new_vectors_first: float32 [6144], replicated
- new_vectors_second: float32 [6144], replicated
- new_table: float32 [16, 169], replicated
- new_table_first: float32 [16, 169], replicated
- new_table_second: float32 [16, 169], replicated
Inputs may be any that keep to these rules, and one draw needn't show every extreme that they name: `regions`: label at (i, j) is 2 * 4 * u + v with u = 2 (i // 7) + (1 if i mod 7 is at least a cut of that row of windows, else 0), v likewise from j and a cut of that column of windows. Each row and column of windows has its own cut; cuts of the first and last ones lie in 1 to 6, the others in 0 to 6. `rel_index`: entry (p, q) depends only on the offset between window positions p and q (position 7 r + c); distinct offsets have distinct entries. `vectors`: the two norms' gains lie in 0.6 to 1.4; the biases in -0.6 to 0.6.
All inputs are finite; a program needn't handle non-finite values.
Results may differ from a plain program's by a relative error of at most 0.02.
Values may be sent and summed in bfloat16 or wider, within the bound.
A program may use at most 128 MiB of HBM per device.

v0:
```python
import jax
import jax.numpy as jnp
from jax import lax
from jax.sharding import PartitionSpec as P

HEAD_DIM = 32
WIN = 7
SHIFT = 3
STEP = 10


norm_eps = 1e-05
mask_fill = -100.0
beta_first = 0.9
beta_second = 0.999
adam_eps = 1e-08
matrix_rate = 0.05
vector_rate = 0.3
matrix_decay = 0.05
root_half = 0.7071067811865476
root_two_pi = 0.3989422804014327


def passed_along(block, axis, distance):
    devices = range(lax.axis_size(axis))
    route = [((i - distance) % len(devices), i) for i in devices]
    return lax.ppermute(block, axis, route)


def layer_norm(values, gain, offset):
    centred = values - jnp.mean(values, axis=-1, keepdims=True)
    inverse = lax.rsqrt(jnp.mean(centred * centred, axis=-1, keepdims=True) + norm_eps)
    normal = centred * inverse
    return (normal * gain + offset, normal, inverse)


def norm_back(grad_in, normal, inverse, gain):
    scaled = grad_in * gain
    centre = jnp.mean(scaled, axis=-1, keepdims=True)
    along = jnp.mean(scaled * normal, axis=-1, keepdims=True)
    return inverse * (scaled - centre - normal * along)


def to_windows(tensor):
    images, rows, columns, channels = tensor.shape
    blocks = tensor.reshape(images, rows, columns // WIN, WIN, channels)
    return blocks.transpose(0, 2, 1, 3, 4).reshape(images, columns // WIN, rows * WIN, channels)


def from_windows(tensor, rows):
    images, window_count, positions, channels = tensor.shape
    blocks = tensor.reshape(images, window_count, rows, WIN, channels)
    return blocks.transpose(0, 2, 1, 3, 4).reshape(images, rows, window_count * WIN, channels)


def split_heads(tensor, heads):
    return tensor.reshape(tensor.shape[:3] + (heads, tensor.shape[-1] // heads))


def window_scores(queries, keys_in, position_bias, mask_bias):
    raw = jnp.einsum("bwihd,bwjhd->bwhij", queries, keys_in, preferred_element_type=jnp.float32)
    return raw * HEAD_DIM ** (-0.5) + position_bias[None, None] + mask_bias[None, :, None]


def adam_step(param, first, second, grad, rate, decay):
    new_first = beta_first * first + (1.0 - beta_first) * grad
    new_second = beta_second * second + (1.0 - beta_second) * grad * grad
    first_hat = new_first / (1.0 - beta_first**STEP)
    second_hat = new_second / (1.0 - beta_second**STEP)
    new_param = param - rate * (first_hat / (jnp.sqrt(second_hat) + adam_eps) + decay * param)
    return (new_param, new_first, new_second)


def local(
    inputs,
    out_grad,
    regions,
    rel_index,
    qkv_weight,
    qkv_first,
    qkv_second,
    proj_weight,
    proj_first,
    proj_second,
    up_weight,
    up_first,
    up_second,
    down_weight,
    down_first,
    down_second,
    vectors,
    vectors_first,
    vectors_second,
    bias_table,
    table_first,
    table_second,
):
    image_count, band_rows, band_cols, model_width = inputs.shape
    hidden_width = up_weight.shape[1]
    head_count = model_width // HEAD_DIM
    window_cols = band_cols // WIN
    kept_rows = band_rows - SHIFT
    token_count = image_count * band_rows * band_cols
    gain_one = vectors[0:model_width]
    shift_one = vectors[model_width : 2 * model_width]
    query_bias = vectors[2 * model_width : 3 * model_width]
    value_bias = vectors[3 * model_width : 4 * model_width]
    proj_bias = vectors[4 * model_width : 5 * model_width]
    gain_two = vectors[5 * model_width : 6 * model_width]
    shift_two = vectors[6 * model_width : 7 * model_width]
    down_bias = vectors[7 * model_width : 8 * model_width]
    up_bias = vectors[8 * model_width : 8 * model_width + hidden_width]
    full_qkv, full_proj, full_up, full_down = (
        lax.all_gather(qkv_weight.astype(jnp.bfloat16), "fsdp", axis=0, tiled=True),
        lax.all_gather(proj_weight.astype(jnp.bfloat16), "fsdp", axis=0, tiled=True),
        lax.all_gather(up_weight.astype(jnp.bfloat16), "fsdp", axis=0, tiled=True),
        lax.all_gather(down_weight.astype(jnp.bfloat16), "fsdp", axis=0, tiled=True),
    )
    flat_in = inputs.reshape(token_count, model_width)
    normed_one, normal_one, inverse_one = layer_norm(flat_in, gain_one, shift_one)
    act_one = normed_one.astype(jnp.bfloat16)
    qkv_bias = jnp.concatenate([query_bias, jnp.zeros_like(query_bias), value_bias])
    qkv_vals = (jnp.dot(act_one, full_qkv, preferred_element_type=jnp.float32) + qkv_bias).astype(
        jnp.bfloat16
    )
    qkv_band = qkv_vals.reshape(image_count, band_rows, band_cols, 3 * model_width)
    below = passed_along(qkv_band[:, :SHIFT], "seq", -1)
    qkv_windows = to_windows(
        jnp.roll(jnp.concatenate([qkv_band[:, SHIFT:], below], axis=1), -SHIFT, axis=2)
    )
    queries = split_heads(qkv_windows[..., 0:model_width], head_count)
    keys_in = split_heads(qkv_windows[..., model_width : 2 * model_width], head_count)
    values_in = split_heads(qkv_windows[..., 2 * model_width : 3 * model_width], head_count)
    pairs = rel_index.shape[0]
    table_size = bias_table.shape[1]
    one_hot = (
        rel_index.reshape(-1)[:, None] == jnp.arange(table_size, dtype=jnp.int32)[None, :]
    ).astype(jnp.float32)
    position_bias = jnp.dot(bias_table, one_hot.T, precision=lax.Precision.HIGHEST).reshape(
        head_count, pairs, pairs
    )
    labels = (
        regions.reshape(band_rows, window_cols, WIN).transpose(1, 0, 2).reshape(window_cols, pairs)
    )
    mask_bias = jnp.where(labels[:, :, None] == labels[:, None, :], 0.0, mask_fill).astype(
        jnp.float32
    )
    scores = window_scores(queries, keys_in, position_bias, mask_bias)
    peak = jnp.max(scores, axis=-1, keepdims=True)
    log_total = peak + jnp.log(jnp.sum(jnp.exp(scores - peak), axis=-1, keepdims=True))
    probs_low = jnp.exp(scores - log_total).astype(jnp.bfloat16)
    attended = jnp.einsum(
        "bwhij,bwjhd->bwihd", probs_low, values_in, preferred_element_type=jnp.float32
    )
    attended_low = attended.astype(jnp.bfloat16).reshape(
        image_count, window_cols, pairs, model_width
    )
    attn_band = jnp.roll(from_windows(attended_low, band_rows), SHIFT, axis=2)
    above = passed_along(attn_band[:, kept_rows:], "seq", 1)
    attn_own = jnp.concatenate([above, attn_band[:, :kept_rows]], axis=1).reshape(
        token_count, model_width
    )
    mid = flat_in + (jnp.dot(attn_own, full_proj, preferred_element_type=jnp.float32) + proj_bias)
    normed_two, normal_two, inverse_two = layer_norm(mid, gain_two, shift_two)
    act_two = normed_two.astype(jnp.bfloat16)
    hidden = jnp.dot(act_two, full_up, preferred_element_type=jnp.float32) + up_bias
    gelu_low = jax.nn.gelu(hidden, approximate=False).astype(jnp.bfloat16)
    block_out = mid + (jnp.dot(gelu_low, full_down, preferred_element_type=jnp.float32) + down_bias)
    grad_flat = out_grad.reshape(token_count, model_width)
    grad_low = grad_flat.astype(jnp.bfloat16)
    down_grad = jnp.dot(gelu_low.T, grad_low, preferred_element_type=jnp.float32)
    down_bias_grad = jnp.sum(grad_low.astype(jnp.float32), axis=0)
    slope = (
        0.5 * (1.0 + lax.erf(hidden * root_half))
        + hidden * jnp.exp(-0.5 * hidden * hidden) * root_two_pi
    )
    hidden_grad = (
        jnp.dot(grad_low, full_down.T, preferred_element_type=jnp.float32) * slope
    ).astype(jnp.bfloat16)
    up_grad = jnp.dot(act_two.T, hidden_grad, preferred_element_type=jnp.float32)
    up_bias_grad = jnp.sum(hidden_grad.astype(jnp.float32), axis=0)
    act_two_grad = jnp.dot(hidden_grad, full_up.T, preferred_element_type=jnp.float32)
    gain_two_grad = jnp.sum(act_two_grad * normal_two, axis=0)
    shift_two_grad = jnp.sum(act_two_grad, axis=0)
    mid_grad = grad_flat + norm_back(act_two_grad, normal_two, inverse_two, gain_two)
    mid_low = mid_grad.astype(jnp.bfloat16)
    proj_grad = jnp.dot(attn_own.T, mid_low, preferred_element_type=jnp.float32)
    proj_bias_grad = jnp.sum(mid_low.astype(jnp.float32), axis=0)
    attn_grad = jnp.dot(mid_low, full_proj.T, preferred_element_type=jnp.float32).astype(
        jnp.bfloat16
    )
    attn_grad = attn_grad.reshape(image_count, band_rows, band_cols, model_width)
    below_grad = passed_along(attn_grad[:, :SHIFT], "seq", -1)
    grad_windows = to_windows(
        jnp.roll(jnp.concatenate([attn_grad[:, SHIFT:], below_grad], axis=1), -SHIFT, axis=2)
    )
    grad_heads = split_heads(grad_windows, head_count)
    scores_again = window_scores(queries, keys_in, position_bias, mask_bias)
    probs = jnp.exp(scores_again - log_total)
    probs_again = probs.astype(jnp.bfloat16)
    value_grad = jnp.einsum(
        "bwhij,bwihd->bwjhd", probs_again, grad_heads, preferred_element_type=jnp.float32
    )
    prob_grad = jnp.einsum(
        "bwihd,bwjhd->bwhij", grad_heads, values_in, preferred_element_type=jnp.float32
    )
    score_grad = (probs * (prob_grad - jnp.sum(probs * prob_grad, axis=-1, keepdims=True))).astype(
        jnp.bfloat16
    )
    score_total = jnp.sum(score_grad.astype(jnp.float32), axis=(0, 1)).reshape(
        head_count, pairs * pairs
    )
    table_grad = jnp.dot(score_total, one_hot, precision=lax.Precision.HIGHEST)
    query_grad = jnp.einsum(
        "bwhij,bwjhd->bwihd", score_grad, keys_in, preferred_element_type=jnp.float32
    ) * HEAD_DIM ** (-0.5)
    key_grad = jnp.einsum(
        "bwhij,bwihd->bwjhd", score_grad, queries, preferred_element_type=jnp.float32
    ) * HEAD_DIM ** (-0.5)
    flat_shape = (image_count, window_cols, pairs, model_width)
    stacked = jnp.concatenate(
        [
            query_grad.reshape(flat_shape),
            key_grad.reshape(flat_shape),
            value_grad.reshape(flat_shape),
        ],
        axis=-1,
    ).astype(jnp.bfloat16)
    qkv_grad_band = jnp.roll(from_windows(stacked, band_rows), SHIFT, axis=2)
    above_grad = passed_along(qkv_grad_band[:, kept_rows:], "seq", 1)
    qkv_grad = jnp.concatenate([above_grad, qkv_grad_band[:, :kept_rows]], axis=1).reshape(
        token_count, 3 * model_width
    )
    qkv_weight_grad = jnp.dot(act_one.T, qkv_grad, preferred_element_type=jnp.float32)
    bias_sums = jnp.sum(qkv_grad.astype(jnp.float32), axis=0)
    act_one_grad = jnp.dot(qkv_grad, full_qkv.T, preferred_element_type=jnp.float32)
    gain_one_grad = jnp.sum(act_one_grad * normal_one, axis=0)
    shift_one_grad = jnp.sum(act_one_grad, axis=0)
    input_grad = mid_grad + norm_back(act_one_grad, normal_one, inverse_one, gain_one)
    owned = (
        lax.psum_scatter(
            qkv_weight_grad.astype(jnp.bfloat16), "fsdp", scatter_dimension=0, tiled=True
        ).astype(jnp.float32),
        lax.psum_scatter(
            proj_grad.astype(jnp.bfloat16), "fsdp", scatter_dimension=0, tiled=True
        ).astype(jnp.float32),
        lax.psum_scatter(
            up_grad.astype(jnp.bfloat16), "fsdp", scatter_dimension=0, tiled=True
        ).astype(jnp.float32),
        lax.psum_scatter(
            down_grad.astype(jnp.bfloat16), "fsdp", scatter_dimension=0, tiled=True
        ).astype(jnp.float32),
    )
    reduced = (
        lax.psum(owned[0].astype(jnp.bfloat16), "seq").astype(jnp.float32),
        lax.psum(owned[1].astype(jnp.bfloat16), "seq").astype(jnp.float32),
        lax.psum(owned[2].astype(jnp.bfloat16), "seq").astype(jnp.float32),
        lax.psum(owned[3].astype(jnp.bfloat16), "seq").astype(jnp.float32),
    )
    vector_grad = jnp.concatenate(
        [
            gain_one_grad,
            shift_one_grad,
            bias_sums[0:model_width],
            bias_sums[2 * model_width : 3 * model_width],
            proj_bias_grad,
            gain_two_grad,
            shift_two_grad,
            down_bias_grad,
            up_bias_grad,
        ]
    )
    vector_sum, table_sum = lax.psum((vector_grad, table_grad), ("seq", "fsdp"))
    qkv_new = adam_step(qkv_weight, qkv_first, qkv_second, reduced[0], matrix_rate, matrix_decay)
    proj_new = adam_step(
        proj_weight, proj_first, proj_second, reduced[1], matrix_rate, matrix_decay
    )
    up_new = adam_step(up_weight, up_first, up_second, reduced[2], matrix_rate, matrix_decay)
    down_new = adam_step(
        down_weight, down_first, down_second, reduced[3], matrix_rate, matrix_decay
    )
    vector_new = adam_step(vectors, vectors_first, vectors_second, vector_sum, vector_rate, 0.0)
    table_new = adam_step(bias_table, table_first, table_second, table_sum, vector_rate, 0.0)
    return (
        block_out.reshape(inputs.shape),
        input_grad.reshape(inputs.shape),
        qkv_new[0],
        qkv_new[1],
        qkv_new[2],
        proj_new[0],
        proj_new[1],
        proj_new[2],
        up_new[0],
        up_new[1],
        up_new[2],
        down_new[0],
        down_new[1],
        down_new[2],
        vector_new[0],
        vector_new[1],
        vector_new[2],
        table_new[0],
        table_new[1],
        table_new[2],
    )


def solution(mesh):
    placed = (
        P("fsdp", "seq", None, None),
        P("fsdp", "seq", None, None),
        P("seq", None),
        P(),
        P("fsdp", None),
        P("fsdp", None),
        P("fsdp", None),
        P("fsdp", None),
        P("fsdp", None),
        P("fsdp", None),
        P("fsdp", None),
        P("fsdp", None),
        P("fsdp", None),
        P("fsdp", None),
        P("fsdp", None),
        P("fsdp", None),
        P(),
        P(),
        P(),
        P(),
        P(),
        P(),
    )
    return jax.shard_map(
        local,
        mesh=mesh,
        in_specs=placed,
        out_specs=(
            P("fsdp", "seq", None, None),
            P("fsdp", "seq", None, None),
            P("fsdp", None),
            P("fsdp", None),
            P("fsdp", None),
            P("fsdp", None),
            P("fsdp", None),
            P("fsdp", None),
            P("fsdp", None),
            P("fsdp", None),
            P("fsdp", None),
            P("fsdp", None),
            P("fsdp", None),
            P("fsdp", None),
            P(),
            P(),
            P(),
            P(),
            P(),
            P(),
        ),
        check_vma=False,
    )
```

profile of v0, /device:TPU:0, one launch (start us, length us, event | category | flops | bytes accessed | tf_op | source)
XLA Modules:
  0.0 400.1 jit_solution(7476023284687217368)
XLA Ops:
  14.4 18.2 %all-gather.4.cloned.1.call-done = bf16[512,1536]{1,0:T(8,128)(2,1)} async-done(((bf16[128,1536]{1,0:T(8,128)(2,1)}), bf16[512,1536]{1,0:T(8,128)(2,1)}) %all-gather.4.cloned.1.call-update) | async-done | bytes 1572880 | tf_op jit(solution)/shard_map/all_gather | solution.py:114
  32.6 3.3 fusion.17
  39.5 4.2 %collective-permute-start = (bf16[2,3,28,1536]{3,0,2,1:T(2,128)(2,1)}, bf16[2,3,28,1536]{3,0,2,1:T(2,128)(2,1)}, u32[]{:S(2)}, u32[]{:S(2)}) collective-permute-start(bf16[2,3,28,1536]{3,0,2,1:T(2,128)(2,1)} %copy.128), channel_id=1, source_target_pairs={{4,0},{8,4},{12,8},{16,12},{20,16},{24,20},{28,24},{0,28},{5,1},{9... | collective-permute-start | bytes 1548296 | tf_op jit(solution)/shard_map/ppermute | solution.py:27
  66.5 3.1 fusion.67
  73.0 4.6 %copy.138 = bf16[2,4,49,16,32]{4,3,1,2,0:T(8,128)(2,1)} copy(bf16[2,4,49,16,32]{2,4,3,1,0:T(8,128)(2,1)} %fusion.22) | data formatting | bytes 802816 | tf_op jit(solution)/shard_map/convert_element_type | solution.py:155
  81.2 8.0 %all_gather.13 = bf16[512,512]{1,0:T(8,128)(2,1)} all-gather(bf16[128,512]{1,0:T(8,128)(2,1)} %convert_element_type.113), channel_id=1, replica_groups=mesh['seq'=8,'fsdp'=4] {'fsdp'}, dimensions={0}, use_global_device_ids=true | all-gather | bytes 655360 | tf_op jit(solution)/shard_map/all_gather | solution.py:115
  93.3 10.4 %fusion.2 = (bf16[392,2048]{1,0:T(8,128)(2,1)}, f32[392,2048]{1,0:T(8,128)}) fusion(f32[2048]{0:T(1024)S(1)} %copy-done.53, bf16[512,2048]{1,0:T(8,128)(2,1)} %all-gather.6.cloned.1.call-done, f32[392,512]{1,0:T(8,128)S(1)} %get-tuple-element.152, f32[512]{0:T(512)S(1)} %copy-done.60, f32[512]{0:T(512)S(1)} %copy-done.49, f32[392]{0:T(512)S(1)} %add_rsqrt_fusion.1, ...), kind=kOutput, calls=%fused_computation.12 | convolution fusion | flops 876072960 | bytes 7732288 | tf_op jit(solution)/shard_map/dot_general | solution.py:166
  103.7 4.5 %convert_reduce_fusion.1 = (f32[2048]{0:T(1024)S(1)}, bf16[392,2048]{1,0:T(8,128)(2,1)S(1)}) fusion(f32[392,2048]{1,0:T(8,128)} %get-tuple-element.154, f32[2048]{0:T(1024)S(1)} %copy-done.53, bf16[2048,512]{1,0:T(8,128)(2,1)} %all-gather.8.cloned.1.call-done, f32[392,512]{1,0:T(8,128)S(1)} %copy-done.17), kind=kOutput, calls=%fused_computation.19 | convolution fusion | flops 832718848 | bytes 7733248 | tf_op jit(solution)/shard_map/dot_general | solution.py:178
  113.0 3.8 collective-permute-start.2
  116.8 4.7 %collective-permute-done.2 = bf16[2,3,28,512]{3,2,1,0:T(8,128)(2,1)S(1)} collective-permute-done((bf16[2,3,28,512]{3,2,1,0:T(8,128)(2,1)S(1)}, bf16[2,3,28,512]{3,2,1,0:T(8,128)(2,1)S(1)}, u32[]{:S(2)}, u32[]{:S(2)}) %collective-permute-start.2) | collective-permute-done | bytes 172064 | tf_op jit(solution)/shard_map/ppermute | solution.py:27
  124.1 3.9 copy.144
  128.0 4.5 %fusion.23 = bf16[2,4,49,16,32]{2,4,3,1,0:T(8,128)(2,1)} fusion(bf16[2,4,49,16,32]{2,4,3,1,0:T(8,128)(2,1)} %copy.144, f32[2,4,16,49,49]{3,4,2,1,0:T(8,128)} %copy-done, f32[2,4,16,49]{3,2,1,0:T(8,128)S(1)} %log_add_fusion), kind=kOutput, calls=%fused_computation.56 | convolution fusion | flops 20484352 | bytes 2057216 | tf_op jit(solution)/shard_map/bwhij,bwihd->bwjhd/dot_general | solution.py:201
  139.8 3.9 copy.151
  145.7 3.9 copy.146
  151.6 4.3 %copy.148 = bf16[2,4,49,16,32]{4,3,1,2,0:T(8,128)(2,1)S(1)} copy(bf16[2,4,49,16,32]{2,4,3,1,0:T(8,128)(2,1)} %fusion.25) | data formatting | bytes 802816 | tf_op jit(solution)/shard_map/mul | solution.py:217
  165.3 14.9 %collective-permute-done.3 = bf16[2,3,28,1536]{3,0,2,1:T(2,128)(2,1)} collective-permute-done((bf16[2,3,28,1536]{3,0,2,1:T(2,128)(2,1)}, bf16[2,3,28,1536]{3,0,2,1:T(2,128)(2,1)}, u32[]{:S(2)}, u32[]{:S(2)}) %collective-permute-start.3) | collective-permute-done | bytes 516128 | tf_op jit(solution)/shard_map/ppermute | solution.py:27
  185.2 4.1 %convolution_convert_fusion = bf16[2048,512]{1,0:T(8,128)(2,1)} fusion(bf16[392,2048]{1,0:T(8,128)(2,1)} %get-tuple-element.153, f32[392,512]{1,0:T(8,128)S(1)} %copy-done.19), kind=kOutput, calls=%fused_computation.37 | convolution fusion | flops 823332864 | bytes 4505600 | tf_op jit(solution)/shard_map/dot_general | solution.py:171
  189.5 4.2 %convolution_convert_fusion.1 = bf16[512,2048]{1,0:T(8,128)(2,1)} fusion(bf16[392,2048]{1,0:T(8,128)(2,1)} %copy-done.63, f32[392,512]{1,0:T(8,128)S(1)} %copy-done.7, f32[512]{0:T(512)S(1)} %copy-done.61, f32[512]{0:T(512)S(1)} %copy-done.49, f32[392]{0:T(512)S(1)} %add_rsqrt_fusion.1, f32[392]{0:T(512)S(1)} %broadcast_multiply_fusion.5), kind=kOutput, calls=%fused_computation.38 | convolution fusion | flops 824135680 | bytes 4512832 | tf_op jit(solution)/shard_map/dot_general | solution.py:180
  194.2 4.0 fusion.27
  213.5 5.9 %reduce-scatter.5.cloned.1.call-done = bf16[128,1536]{1,0:T(8,128)(2,1)} async-done(((bf16[512,1536]{1,0:T(8,128)(2,1)}), bf16[128,1536]{1,0:T(8,128)(2,1)}) %reduce-scatter.5.cloned.1.call-update) | async-done | bytes 393232 | tf_op jit(solution)/shard_map/reduce_scatter | solution.py:241
  219.4 33.8 %reduce-scatter.11.cloned.1.call-done = bf16[512,512]{1,0:T(8,128)(2,1)} async-done(((bf16[2048,512]{1,0:T(8,128)(2,1)}), bf16[512,512]{1,0:T(8,128)(2,1)}) %reduce-scatter.11.cloned.1.call-update) | async-done | bytes 524304 | tf_op jit(solution)/shard_map/reduce_scatter | solution.py:250
  253.2 34.2 %reduce-scatter.9.cloned.1.call-done = bf16[128,2048]{1,0:T(8,128)(2,1)} async-done(((bf16[512,2048]{1,0:T(8,128)(2,1)}), bf16[128,2048]{1,0:T(8,128)(2,1)}) %reduce-scatter.9.cloned.1.call-update) | async-done | bytes 524304 | tf_op jit(solution)/shard_map/reduce_scatter | solution.py:247
  287.5 41.8 %all-reduce = (f32[6144]{0:T(1024)S(1)}, f32[16,169]{1,0:T(8,128)S(1)}) all-reduce(f32[6144]{0:T(1024)S(1)} %constant_dynamic-update-slice_fusion, f32[16,169]{1,0:T(8,128)S(1)} %fusion.19), channel_id=1, replica_groups=mesh['seq'=8,'fsdp'=4] {'seq','fsdp'}, use_global_device_ids=true, to_apply=%region_27.28 | all-reduce | flops 8848 | bytes 70784 | tf_op jit(solution)/shard_map/psum | solution.py:273
  330.7 51.8 %all-reduce.4.cloned.1.call-done = (bf16[128,1536]{1,0:T(8,128)(2,1)}, bf16[128,512]{1,0:T(8,128)(2,1)}, bf16[128,2048]{1,0:T(8,128)(2,1)}, bf16[512,512]{1,0:T(8,128)(2,1)}) async-done(((bf16[128,1536]{1,0:T(8,128)(2,1)}, bf16[128,512]{1,0:T(8,128)(2,1)}, bf16[128,2048]{1,0:T(8,128)(2,1)}, bf16[512,512]{1,0:T(8,128)(2,1)}), (bf16[128,1536]{1,0:T(8,128)(2,1)}, bf16[128,512]{1,0:T(8,128)(2,1)}, ...) | async-done | bytes 1572880 | tf_op jit(solution)/shard_map/psum | solution.py:255
  (268 shorter events, 104.5 us)
Async XLA Ops:
  7.2 25.4 %all-gather.4.cloned.1.call-start = ((), (), s32[]{:S(2)}) async-start(), calls=%async_computation.4 | async-start | bytes 1966080 | tf_op jit(solution)/shard_map/all_gather | solution.py:114
  9.3 84.0 %all-gather.6.cloned.1.call-start = ((), (), s32[]{:S(2)}) async-start(), calls=%async_computation.5 | async-start | bytes 2621440 | tf_op jit(solution)/shard_map/all_gather | solution.py:116
  11.4 92.3 %all-gather.8.cloned.1.call-start = ((), (), s32[]{:S(2)}) async-start(), calls=%async_computation.6 | async-start | bytes 2621440 | tf_op jit(solution)/shard_map/all_gather | solution.py:117
  13.7 77.6 %copy-start.8 = (f32[392,512]{1,0:T(8,128)}, f32[392,512]{1,0:T(8,128)S(1)}, u32[]{:S(2)}) copy-start(f32[392,512]{1,0:T(8,128)S(1)} %reshape.210) | copy-start | bytes 2408452
  39.5 17.9 %collective-permute-start = (bf16[2,3,28,1536]{3,0,2,1:T(2,128)(2,1)}, bf16[2,3,28,1536]{3,0,2,1:T(2,128)(2,1)}, u32[]{:S(2)}, u32[]{:S(2)}) collective-permute-start(bf16[2,3,28,1536]{3,0,2,1:T(2,128)(2,1)} %copy.128), channel_id=1, source_target_pairs={{4,0},{8,4},{12,8},{16,12},{20,16},{24,20},{28,24},{0,28},{5,1},{9... | collective-permute-start | bytes 1548296 | tf_op jit(solution)/shard_map/ppermute | solution.py:27
  45.8 167.7 %reduce-scatter.7.cloned.1.call-start = ((), (), s32[]{:S(2)}) async-start(), calls=%async_computation.8 | async-start | bytes 655360 | tf_op jit(solution)/shard_map/reduce_scatter | solution.py:244
  81.1 8.7 %collective-permute-start.1 = (bf16[2,3,28,512]{3,0,2,1:T(2,128)(2,1)S(1)}, bf16[2,3,28,512]{3,0,2,1:T(2,128)(2,1)S(1)}, u32[]{:S(2)}, u32[]{:S(2)}) collective-permute-start(bf16[2,3,28,512]{3,0,2,1:T(2,128)(2,1)S(1)} %pad_maximum_fusion.5), channel_id=1, source_target_pairs={{28,0},{0,4},{4,8},{8,12},{12,16},{16,20},{20,24},{24,28},{29,1},{... | collective-permute-start | bytes 516104 | tf_op jit(solution)/shard_map/ppermute | solution.py:27
  113.0 8.5 %collective-permute-start.2 = (bf16[2,3,28,512]{3,2,1,0:T(8,128)(2,1)S(1)}, bf16[2,3,28,512]{3,2,1,0:T(8,128)(2,1)S(1)}, u32[]{:S(2)}, u32[]{:S(2)}) collective-permute-start(bf16[2,3,28,512]{3,2,1,0:T(8,128)(2,1)S(1)} %slice.138), channel_id=1, source_target_pairs={{4,0},{8,4},{12,8},{16,12},{20,16},{24,20},{28,24},{0,28},{5,1},{9... | collective-permute-start | bytes 516104 | tf_op jit(solution)/shard_map/ppermute | solution.py:27
  163.3 16.9 %collective-permute-start.3 = (bf16[2,3,28,1536]{3,0,2,1:T(2,128)(2,1)}, bf16[2,3,28,1536]{3,0,2,1:T(2,128)(2,1)}, u32[]{:S(2)}, u32[]{:S(2)}) collective-permute-start(bf16[2,3,28,1536]{3,0,2,1:T(2,128)(2,1)} %copy.155), channel_id=1, source_target_pairs={{28,0},{0,4},{4,8},{8,12},{12,16},{16,20},{20,24},{24,28},{29,1},{... | collective-permute-start | bytes 1548296 | tf_op jit(solution)/shard_map/ppermute | solution.py:27
  164.6 54.8 %reduce-scatter.5.cloned.1.call-start = ((), (), s32[]{:S(2)}) async-start(), calls=%async_computation.7 | async-start | bytes 1966080 | tf_op jit(solution)/shard_map/reduce_scatter | solution.py:241
  185.1 68.1 %reduce-scatter.11.cloned.1.call-start = ((), (), s32[]{:S(2)}) async-start(), calls=%async_computation.10 | async-start | bytes 2621440 | tf_op jit(solution)/shard_map/reduce_scatter | solution.py:250
  189.4 98.0 %reduce-scatter.9.cloned.1.call-start = ((), (), s32[]{:S(2)}) async-start(), calls=%async_computation.9 | async-start | bytes 2621440 | tf_op jit(solution)/shard_map/reduce_scatter | solution.py:247
  193.7 188.8 %all-reduce.4.cloned.1.call-start = ((), (), s32[]{:S(2)}) async-start(), calls=%async_computation.11 | async-start | bytes 3145728 | tf_op jit(solution)/shard_map/psum | solution.py:255
  211.8 117.6 %copy-start.44 = (f32[16,169]{1,0:T(8,128)S(1)}, f32[16,169]{1,0:T(8,128)}, u32[]{:S(2)}) copy-start(f32[16,169]{1,0:T(8,128)} %param.41) | copy-start | bytes 32452
  211.8 117.6 %copy-start.45 = (f32[16,169]{1,0:T(8,128)S(1)}, f32[16,169]{1,0:T(8,128)}, u32[]{:S(2)}) copy-start(f32[16,169]{1,0:T(8,128)} %param.42) | copy-start | bytes 32452
  211.8 117.6 %copy-start.46 = (f32[16,169]{1,0:T(8,128)S(1)}, f32[16,169]{1,0:T(8,128)}, u32[]{:S(2)}) copy-start(f32[16,169]{1,0:T(8,128)} %param.43) | copy-start | bytes 32452
  211.8 118.2 %copy-start.37 = (f32[6144]{0:T(1024)S(1)}, f32[6144]{0:T(1024)}, u32[]{:S(2)}) copy-start(f32[6144]{0:T(1024)} %param.38) | copy-start | bytes 73732
  211.8 118.2 %copy-start.39 = (f32[6144]{0:T(1024)S(1)}, f32[6144]{0:T(1024)}, u32[]{:S(2)}) copy-start(f32[6144]{0:T(1024)} %param.39) | copy-start | bytes 73732
  211.8 118.2 %copy-start.40 = (f32[6144]{0:T(1024)S(1)}, f32[6144]{0:T(1024)}, u32[]{:S(2)}) copy-start(f32[6144]{0:T(1024)} %param.40) | copy-start | bytes 73732
  211.8 170.7 %copy-start.24 = (f32[128,512]{1,0:T(8,128)S(1)}, f32[128,512]{1,0:T(8,128)}, u32[]{:S(2)}) copy-start(f32[128,512]{1,0:T(8,128)} %param.29) | copy-start | bytes 786436
  211.8 170.7 %copy-start.34 = (f32[128,512]{1,0:T(8,128)S(1)}, f32[128,512]{1,0:T(8,128)}, u32[]{:S(2)}) copy-start(f32[128,512]{1,0:T(8,128)} %param.30) | copy-start | bytes 786436
  211.8 170.7 %copy-start.35 = (f32[128,512]{1,0:T(8,128)S(1)}, f32[128,512]{1,0:T(8,128)}, u32[]{:S(2)}) copy-start(f32[128,512]{1,0:T(8,128)} %param.31) | copy-start | bytes 786436
  211.9 172.8 %copy-start.20 = (f32[128,1536]{1,0:T(8,128)S(1)}, f32[128,1536]{1,0:T(8,128)}, u32[]{:S(2)}) copy-start(f32[128,1536]{1,0:T(8,128)} %param.26) | copy-start | bytes 2359300
  212.0 172.7 %copy-start.31 = (f32[128,1536]{1,0:T(8,128)S(1)}, f32[128,1536]{1,0:T(8,128)}, u32[]{:S(2)}) copy-start(f32[128,1536]{1,0:T(8,128)} %param.27) | copy-start | bytes 2359300
  (52 other events, 338.2 us)
Sparse Core Ops, SparseCore 0:
  10.2 22.3 all-gather.3
  34.7 22.5 all-gather.5
  59.5 22.5 all-gather.7
  164.7 23.9 reduce-scatter.6
  191.2 28.1 reduce-scatter.4
  221.8 31.4 reduce-scatter.10
  255.9 31.4 reduce-scatter.8
  291.2 91.2 all-reduce.3
where the time goes:
time: 404 us; the launch traced here: 400 us
  waiting for transfers between devices  164 us (41%)
  local copies, waits for them, and re-layouts  74.4 us (18%)
  matrix products  58.5 us (14%)
  blocking collectives  49.8 us (12%)
  other arithmetic  28.5 us (7%)
  between operations  15.5 us (4%)
  starting transfers between devices  9.11 us (2%)
    psum x1, waiting for transfers between devices, local(): lax.psum(owned[0].astype(jnp.bfloat16), 'seq').astype(jnp.float32)  51.8 us
    psum x1, blocking collectives, local(): vector_sum, table_sum = lax.psum((vector_grad, table_grad), ('seq', 'fsdp'))  41.8 us
    reduce_scatter x1, waiting for transfers between devices, local(): lax.psum_scatter(up_grad.astype(jnp.bfloat16), 'fsdp', scatter_dimension=...  34.2 us
    reduce_scatter x1, waiting for transfers between devices, local(): lax.psum_scatter(down_grad.astype(jnp.bfloat16), 'fsdp', scatter_dimensio...  33.8 us
    ppermute x4, waiting for transfers between devices, passed_along(): return lax.ppermute(block, axis, route)  20.2 us
    all_gather x1, waiting for transfers between devices, local(): lax.all_gather(qkv_weight.astype(jnp.bfloat16), 'fsdp', axis=0, tiled=True)  18.2 us
    unnamed x142, local copies, waits for them, and re-layouts  11.1 us
    sub x6, other arithmetic, adam_step(): param - rate * (first_hat / (jnp.sqrt(second_hat) + adam_eps) + decay * p...  10.8 us
  transfers between devices with their start and end apart: 12, of which 8 were waited for; matrix products, arithmetic and copies ran while one was open for 24% of the time, Pallas kernels for 0%

commit v1 on v0

--- a/solution.py
+++ b/solution.py
@@ -1,6 +1,8 @@
 import jax
 import jax.numpy as jnp
 from jax import lax
+from jax.experimental import pallas as pl
+from jax.experimental.pallas import tpu as pltpu
 from jax.sharding import PartitionSpec as P
 
 HEAD_DIM = 32
@@ -69,6 +71,219 @@
     second_hat = new_second / (1.0 - beta_second**STEP)
     new_param = param - rate * (first_hat / (jnp.sqrt(second_hat) + adam_eps) + decay * param)
     return (new_param, new_first, new_second)
+
+
+def chunk_list(qkv, proj, up, down, width):
+    chunks = []
+    for k in range(down.shape[0] // proj.shape[0]):
+        chunks.append((down, None, k))
+    for k in range(up.shape[1] // width):
+        chunks.append((up, k * width, 0))
+    chunks.append((proj, 0, 0))
+    for k in range(qkv.shape[1] // width):
+        chunks.append((qkv, k * width, 0))
+    return chunks
+
+
+def reduce_kernel(
+    qkv, proj, up, down, vec, o_qkv, o_proj, o_up, o_down, o_vec,
+    from_core, to_x, from_x, to_y, from_y, mine, to_z, from_z,
+    v_keep, v_core, v_x, v_y, v_z,
+    core_send, core_recv, x_send, x_recv, y_send, y_recv, z_send, z_recv,
+    zg_send, zg_recv, yg_send, yg_recv, v_send, v_recv,
+):
+    f32, bf16 = jnp.float32, jnp.bfloat16
+    seq, fsdp = lax.axis_index("seq"), lax.axis_index("fsdp")
+    z, y = seq // 2, seq % 2
+    x, core = fsdp // 2, fsdp % 2
+    sib = {"seq": seq, "fsdp": x * 2 + (1 - core)}
+    across = {"seq": seq, "fsdp": (1 - x) * 2 + core}
+    beside = {"seq": z * 2 + (1 - y), "fsdp": fsdp}
+    others = [(z + d) % 4 for d in (1, 2, 3)]
+    along = [{"seq": o * 2 + y, "fsdp": fsdp} for o in others]
+    barrier = pltpu.get_barrier_semaphore()
+    for dev in [sib, across, beside] + along:
+        pl.semaphore_signal(barrier, inc=1, device_id=dev, device_id_type=pl.DeviceIdType.MESH)
+    pl.semaphore_wait(barrier, 6)
+
+    rows, width = o_proj.shape
+    half, quarter = rows // 2, rows // 8
+    ins = chunk_list(qkv, proj, up, down, width)
+    outs = chunk_list(o_qkv, o_proj, o_up, o_down, width)
+    count = len(ins)
+    sends = []
+
+    def send(src, dst, s_sem, r_sem, dev):
+        copy = pltpu.make_async_remote_copy(
+            src_ref=src, dst_ref=dst, send_sem=s_sem, recv_sem=r_sem,
+            device_id=dev, device_id_type=pl.DeviceIdType.MESH,
+        )
+        copy.start()
+        sends.append(copy)
+        return copy
+
+    def part(c, shard, off, n):
+        ref, col, block = ins[c]
+        if col is None:
+            per = ref.shape[0] // 4
+            return ref.at[pl.ds(pl.multiple_of(shard * per + block * rows + off, 16), n), :]
+        return ref.at[pl.ds(pl.multiple_of(shard * rows + off, 16), n), col : col + width]
+
+    def result(c, off, n):
+        ref, col, block = outs[c]
+        if col is None:
+            return ref.at[pl.ds(pl.multiple_of(block * rows + off, 16), n), :]
+        return ref.at[pl.ds(pl.multiple_of(off, 16), n), col : col + width]
+
+    c_core, c_x, c_y, c_z, c_zg, c_yg = {}, {}, {}, {}, {}, {}
+    vc = [send(vec, v_core, v_send.at[0], v_recv.at[0], sib)]
+    for c in range(count):
+        c_core[c] = [
+            send(part(c, xx * 2 + (1 - core), 0, rows), from_core.at[c, xx],
+                 core_send.at[c, xx], core_recv.at[c, xx], sib)
+            for xx in (0, 1)
+        ]
+
+    def stage_x(c):
+        for copy in c_core[c]:
+            copy.wait_recv()
+        total = part(c, (1 - x) * 2 + core, 0, rows)[...].astype(f32) + from_core[c, 1 - x].astype(f32)
+        to_x[c] = total.astype(bf16)
+        c_x[c] = send(to_x.at[c], from_x.at[c], x_send.at[c], x_recv.at[c], across)
+
+    def three(c, off):
+        here = pl.ds(pl.multiple_of(off, 16), half)
+        return (
+            part(c, x * 2 + core, off, half)[...].astype(f32)
+            + from_core[c, x, here].astype(f32)
+            + from_x[c, here].astype(f32)
+        )
+
+    def stage_y(c):
+        c_x[c].wait_recv()
+        to_y[c] = three(c, (1 - y) * half).astype(bf16)
+        c_y[c] = send(to_y.at[c], from_y.at[c], y_send.at[c], y_recv.at[c], beside)
+
+    def stage_z(c):
+        c_y[c].wait_recv()
+        total = three(c, y * half) + from_y[c].astype(f32)
+        mine[c] = total
+        to_z[c] = total.astype(bf16)
+        c_z[c] = [
+            send(to_z.at[c, pl.ds(pl.multiple_of(others[d] * quarter, 16), quarter)], from_z.at[c, d],
+                 z_send.at[c, d], z_recv.at[c, d], along[d])
+            for d in range(3)
+        ]
+
+    def stage_sum(c):
+        for copy in c_z[c]:
+            copy.wait_recv()
+        total = mine[c, pl.ds(pl.multiple_of(z * quarter, 16), quarter)]
+        for d in range(3):
+            total = total + from_z[c, d].astype(f32)
+        place = result(c, y * half + z * quarter, quarter)
+        place[...] = total.astype(bf16)
+        c_zg[c] = [
+            send(place, place, zg_send.at[c, d], zg_recv.at[c, d], along[d]) for d in range(3)
+        ]
+
+    def stage_back(c):
+        for copy in c_zg[c]:
+            copy.wait_recv()
+        place = result(c, y * half, half)
+        c_yg[c] = send(place, place, yg_send.at[c], yg_recv.at[c], beside)
+
+    def stage_end(c):
+        c_yg[c].wait_recv()
+
+    def vec_step(i):
+        if i == 0:
+            vc[0].wait_recv()
+            v_keep[0] = vec[...] + v_core[...]
+            vc.append(send(v_keep.at[0], v_x, v_send.at[1], v_recv.at[1], across))
+        elif i == 1:
+            vc[1].wait_recv()
+            v_keep[1] = v_keep[0] + v_x[...]
+            vc.append(send(v_keep.at[1], v_y, v_send.at[2], v_recv.at[2], beside))
+        elif i == 2:
+            vc[2].wait_recv()
+            v_z[z] = v_keep[1] + v_y[...]
+            for d in range(3):
+                vc.append(send(v_z.at[z], v_z.at[z], v_send.at[3 + d], v_recv.at[3 + d], along[d]))
+        elif i == 3:
+            for copy in vc[3:]:
+                copy.wait_recv()
+            o_vec[...] = v_z[0] + v_z[1] + v_z[2] + v_z[3]
+
+    vec_step(0)
+    for c in range(count):
+        stage_x(c)
+    stages = [stage_y, stage_z, stage_sum, stage_back, stage_end]
+    for t in range(count + len(stages) - 1):
+        for s, stage in enumerate(stages):
+            if 0 <= t - s < count:
+                stage(t - s)
+        if t in (0, 1, 2):
+            vec_step(t + 1)
+    for copy in sends:
+        copy.wait_send()
+
+
+def reduce_all(qkv, proj, up, down, vec):
+    bf16 = jnp.bfloat16
+    rows, width = proj.shape[0] // 4, proj.shape[1]
+    n = (qkv.size + proj.size + up.size + down.size) // (4 * rows * width)
+    dma = pltpu.SemaphoreType.DMA
+    vmem = pl.BlockSpec(memory_space=pltpu.VMEM)
+    return pl.pallas_call(
+        reduce_kernel,
+        out_shape=[jax.ShapeDtypeStruct((a.shape[0] // 4, a.shape[1]), bf16) for a in (qkv, proj, up, down)]
+        + [jax.ShapeDtypeStruct(vec.shape, jnp.float32)],
+        in_specs=[vmem] * 5,
+        out_specs=[vmem] * 5,
+        scratch_shapes=[
+            pltpu.VMEM((n, 2, rows, width), bf16),
+            pltpu.VMEM((n, rows, width), bf16),
+            pltpu.VMEM((n, rows, width), bf16),
+            pltpu.VMEM((n, rows // 2, width), bf16),
+            pltpu.VMEM((n, rows // 2, width), bf16),
+            pltpu.VMEM((n, rows // 2, width), jnp.float32),
+            pltpu.VMEM((n, rows // 2, width), bf16),
+            pltpu.VMEM((n, 3, rows // 8, width), bf16),
+            pltpu.VMEM((2,) + vec.shape, jnp.float32),
+            pltpu.VMEM(vec.shape, jnp.float32),
+            pltpu.VMEM(vec.shape, jnp.float32),
+            pltpu.VMEM(vec.shape, jnp.float32),
+            pltpu.VMEM((4,) + vec.shape, jnp.float32),
+            dma((n, 2)), dma((n, 2)), dma((n,)), dma((n,)), dma((n,)), dma((n,)),
+            dma((n, 3)), dma((n, 3)), dma((n, 3)), dma((n, 3)), dma((n,)), dma((n,)),
+            dma((6,)), dma((6,)),
+        ],
+        compiler_params=pltpu.CompilerParams(
+            collective_id=0, has_side_effects=True, vmem_limit_bytes=48 * 1024 * 1024
+        ),
+        name="reduce_all",
+    )(qkv, proj, up, down, vec)
+
+
+def summed(qkv, proj, up, down, vector_grad, table_grad):
+    low = [g.astype(jnp.bfloat16) for g in (qkv, proj, up, down)]
+    if lax.axis_size("seq") == 8 and lax.axis_size("fsdp") == 4:
+        size = vector_grad.size + table_grad.size
+        padded = -(-size // 1024) * 1024
+        flat = jnp.concatenate(
+            [vector_grad, table_grad.reshape(-1), jnp.zeros((padded - size,), jnp.float32)]
+        ).reshape(padded // 128, 128)
+        *owned, total = reduce_all(*low, flat)
+        total = total.reshape(-1)
+        vector_sum = total[: vector_grad.size]
+        table_sum = total[vector_grad.size : size].reshape(table_grad.shape)
+    else:
+        owned = [
+            lax.psum(lax.psum_scatter(g, "fsdp", scatter_dimension=0, tiled=True), "seq") for g in low
+        ]
+        vector_sum, table_sum = lax.psum((vector_grad, table_grad), ("seq", "fsdp"))
+    return [g.astype(jnp.float32) for g in owned], vector_sum, table_sum
 
 
 def local(
@@ -237,26 +452,6 @@
     gain_one_grad = jnp.sum(act_one_grad * normal_one, axis=0)
     shift_one_grad = jnp.sum(act_one_grad, axis=0)
     input_grad = mid_grad + norm_back(act_one_grad, normal_one, inverse_one, gain_one)
-    owned = (
-        lax.psum_scatter(
-            qkv_weight_grad.astype(jnp.bfloat16), "fsdp", scatter_dimension=0, tiled=True
-        ).astype(jnp.float32),
-        lax.psum_scatter(
-            proj_grad.astype(jnp.bfloat16), "fsdp", scatter_dimension=0, tiled=True
-        ).astype(jnp.float32),
-        lax.psum_scatter(
-            up_grad.astype(jnp.bfloat16), "fsdp", scatter_dimension=0, tiled=True
-        ).astype(jnp.float32),
-        lax.psum_scatter(
-            down_grad.astype(jnp.bfloat16), "fsdp", scatter_dimension=0, tiled=True
-        ).astype(jnp.float32),
-    )
-    reduced = (
-        lax.psum(owned[0].astype(jnp.bfloat16), "seq").astype(jnp.float32),
-        lax.psum(owned[1].astype(jnp.bfloat16), "seq").astype(jnp.float32),
-        lax.psum(owned[2].astype(jnp.bfloat16), "seq").astype(jnp.float32),
-        lax.psum(owned[3].astype(jnp.bfloat16), "seq").astype(jnp.float32),
-    )
     vector_grad = jnp.concatenate(
         [
             gain_one_grad,
@@ -270,7 +465,9 @@
             up_bias_grad,
         ]
     )
-    vector_sum, table_sum = lax.psum((vector_grad, table_grad), ("seq", "fsdp"))
+    reduced, vector_sum, table_sum = summed(
+        qkv_weight_grad, proj_grad, up_grad, down_grad, vector_grad, table_grad
+    )
     qkv_new = adam_step(qkv_weight, qkv_first, qkv_second, reduced[0], matrix_rate, matrix_decay)
     proj_new = adam_step(
         proj_weight, proj_first, proj_second, reduced[1], matrix_rate, matrix_decay

time: 404 us -> 292 us (0.72)
  waiting for transfers between devices: 164 us -> 29.1 us
  Pallas kernels: 0 us -> 63.2 us
  blocking collectives: 49.8 us -> 10.1 us
  matrix products: 58.5 us -> 51.9 us
  other arithmetic: 28.5 us -> 33.5 us
    reduce_scatter x4 -> x0, waiting for transfers between devices: 73.9 us -> none  [the longest x1 34.2 us: local(): lax.psum_scatter(up_grad.astype(jnp.bfloat16), 'fsdp', scatter_dimension=...]
    pallas_call x0 -> x1, Pallas kernels: none -> 63.2 us  [reduce_all(): pl.pallas_call(reduce_kernel, out_shape=[jax.ShapeDtypeStruct((a.shape[0]...]
    psum x1 -> x0, waiting for transfers between devices: 51.8 us -> none  [local(): lax.psum(owned[0].astype(jnp.bfloat16), 'seq').astype(jnp.float32)]
    psum x1 -> x0, blocking collectives: 41.8 us -> none  [local(): vector_sum, table_sum = lax.psum((vector_grad, table_grad), ('seq', 'fsdp'))]
    ppermute x4, waiting for transfers between devices: 20.2 us -> 11.4 us  [passed_along(): return lax.ppermute(block, axis, route)]
    unnamed x142 -> x138, local copies, waits for them, and re-layouts: 11.1 us -> 13 us
  transfers between devices with their start and end apart: 12 -> 7, of which waited for: 8 -> 3; matrix products, arithmetic and copies ran while one was open for 24% -> 23% of each run, Pallas kernels for 0% -> 0%
where the time goes in v1:
time: 292 us; the launch traced here: 288 us
  local copies, waits for them, and re-layouts  74.9 us (26%)
  Pallas kernels  63.2 us (22%)
  matrix products  51.9 us (18%)
  other arithmetic  33.5 us (11%)
  waiting for transfers between devices  29.1 us (10%)
  between operations  15 us (5%)
  starting transfers between devices  10.4 us (4%)
  blocking collectives  10.1 us (3%)
    pallas_call x1, Pallas kernels, reduce_all(): pl.pallas_call(reduce_kernel, out_shape=[jax.ShapeDtypeStruct((a.shape[0]...  63.2 us
    all_gather x1, waiting for transfers between devices, local(): lax.all_gather(qkv_weight.astype(jnp.bfloat16), 'fsdp', axis=0, tiled=True)  17.7 us
    unnamed x138, local copies, waits for them, and re-layouts  13 us
    ppermute x4, waiting for transfers between devices, passed_along(): return lax.ppermute(block, axis, route)  11.4 us
    dot_general x1, matrix products, local(): jnp.dot(act_two, full_up, preferred_element_type=jnp.float32) + up_bias  10.4 us
    ppermute x4, starting transfers between devices, passed_along(): return lax.ppermute(block, axis, route)  10.3 us
    all_gather x1, blocking collectives, local(): lax.all_gather(proj_weight.astype(jnp.bfloat16), 'fsdp', axis=0, tiled=True)  10.1 us
    sub x6, other arithmetic, adam_step(): param - rate * (first_hat / (jnp.sqrt(second_hat) + adam_eps) + decay * p...  9.81 us
  transfers between devices with their start and end apart: 7, of which 3 were waited for; matrix products, arithmetic and copies ran while one was open for 23% of the time, Pallas kernels for 0%

profile of v1, /device:TPU:0, one launch (start us, length us, event | category | flops | bytes accessed | tf_op | source)
XLA Modules:
  0.0 288.1 jit_solution(4483388499147697651)
XLA Ops:
  14.9 17.7 %all-gather.4.cloned.1.call-done = bf16[512,1536]{1,0:T(8,128)(2,1)} async-done(((bf16[128,1536]{1,0:T(8,128)(2,1)}), bf16[512,1536]{1,0:T(8,128)(2,1)}) %all-gather.4.cloned.1.call-update) | async-done | bytes 1572880 | tf_op jit(solution)/shard_map/all_gather | solution.py:329
  32.6 3.3 %fusion.17 = bf16[392,1536]{1,0:T(8,128)(2,1)} fusion(bf16[512,1536]{1,0:T(8,128)(2,1)} %all-gather.4.cloned.1.call-done, f32[1536]{0:T(1024)S(1)} %pad_maximum_fusion.6, f32[392,512]{1,0:T(8,128)S(1)} %reshape.223, f32[512]{0:T(512)S(1)} %get-tuple-element.151, f32[512]{0:T(512)S(1)} %get-tuple-element.152, f32[392]{0:T(512)S(1)} %rsqrt.21, f32[392]{0:T(512)S(1)} %div.117), kind=kOutput, calls=%fused_computation.39 | convolution fusion | flops 618770432 | bytes 3593280 | tf_op jit(solution)/shard_map/dot_general | solution.py:338
  39.5 4.7 %collective-permute-start = (bf16[2,3,28,1536]{3,0,2,1:T(2,128)(2,1)}, bf16[2,3,28,1536]{3,0,2,1:T(2,128)(2,1)}, u32[]{:S(2)}, u32[]{:S(2)}) collective-permute-start(bf16[2,3,28,1536]{3,0,2,1:T(2,128)(2,1)} %copy.128), channel_id=1, source_target_pairs={{4,0},{8,4},{12,8},{16,12},{20,16},{24,20},{28,24},{0,28},{5,1},{9... | collective-permute-start | bytes 1548296 | tf_op jit(solution)/shard_map/ppermute | solution.py:29
  49.8 6.2 %collective-permute-done = bf16[2,3,28,1536]{3,0,2,1:T(2,128)(2,1)} collective-permute-done((bf16[2,3,28,1536]{3,0,2,1:T(2,128)(2,1)}, bf16[2,3,28,1536]{3,0,2,1:T(2,128)(2,1)}, u32[]{:S(2)}, u32[]{:S(2)}) %collective-permute-start) | collective-permute-done | bytes 516128 | tf_op jit(solution)/shard_map/ppermute | solution.py:29
  67.4 3.0 %copy.138 = bf16[2,4,49,16,32]{4,3,1,2,0:T(8,128)(2,1)S(1)} copy(bf16[2,4,49,16,32]{2,4,3,1,0:T(8,128)(2,1)S(1)} %fusion.22) | data formatting | bytes 802816 | tf_op jit(solution)/shard_map/convert_element_type | solution.py:370
  73.2 10.1 %all_gather.13 = bf16[512,512]{1,0:T(8,128)(2,1)S(1)} all-gather(bf16[128,512]{1,0:T(8,128)(2,1)S(1)} %copy-done.40), channel_id=1, replica_groups=mesh['seq'=8,'fsdp'=4] {'fsdp'}, dimensions={0}, use_global_device_ids=true | all-gather | bytes 655360 | tf_op jit(solution)/shard_map/all_gather | solution.py:330
  89.4 10.4 %fusion.2 = (bf16[392,2048]{1,0:T(8,128)(2,1)}, f32[392,2048]{1,0:T(8,128)}) fusion(f32[2048]{0:T(1024)S(1)} %slice.125, bf16[512,2048]{1,0:T(8,128)(2,1)} %all-gather.6.cloned.1.call-done, f32[392,512]{1,0:T(8,128)S(1)} %get-tuple-element.158, f32[512]{0:T(512)S(1)} %copy-done.59, f32[512]{0:T(512)S(1)} %get-tuple-element.147, ...), kind=kOutput, calls=%fused_computation.12 | convolution fusion | flops 876072960 | bytes 7732288 | tf_op jit(solution)/shard_map/dot_general | solution.py:381
  99.8 4.5 %convert_reduce_fusion.1 = (f32[2048]{0:T(1024)S(1)}, bf16[392,2048]{1,0:T(8,128)(2,1)S(1)}) fusion(f32[392,2048]{1,0:T(8,128)} %get-tuple-element.160, f32[2048]{0:T(1024)S(1)} %slice.125, bf16[2048,512]{1,0:T(8,128)(2,1)} %all-gather.8.cloned.1.call-done, f32[392,512]{1,0:T(8,128)S(1)} %copy-done.27), kind=kOutput, calls=%fused_computation.19 | convolution fusion | flops 832718848 | bytes 7733248 | tf_op jit(solution)/shard_map/dot_general | solution.py:393
  106.6 4.7 %collective-permute-start.2 = (bf16[2,3,28,512]{3,2,1,0:T(8,128)(2,1)S(1)}, bf16[2,3,28,512]{3,2,1,0:T(8,128)(2,1)S(1)}, u32[]{:S(2)}, u32[]{:S(2)}) collective-permute-start(bf16[2,3,28,512]{3,2,1,0:T(8,128)(2,1)S(1)} %slice.150), channel_id=1, source_target_pairs={{4,0},{8,4},{12,8},{16,12},{20,16},{24,20},{28,24},{0,28},{5,1},{9... | collective-permute-start | bytes 516104 | tf_op jit(solution)/shard_map/ppermute | solution.py:29
  111.3 4.1 %fusion.27 = f32[392,512]{1,0:T(8,128)} fusion(f32[392,512]{1,0:T(8,128)S(1)} %get-tuple-element.158, bf16[392,2048]{1,0:T(8,128)(2,1)} %get-tuple-element.159, bf16[2048,512]{1,0:T(8,128)(2,1)} %all-gather.8.cloned.1.call-done, f32[512]{0:T(512)S(1)} %copy-done.60), kind=kOutput, calls=%fused_computation.65 | convolution fusion | flops 822484992 | bytes 5310464 | tf_op jit(solution)/shard_map/dot_general | solution.py:383
  119.5 3.2 %reshape_reshape.7 = bf16[2,4,49,16,32]{4,3,1,2,0:T(8,128)(2,1)} reshape(bf16[2,4,7,7,512]{4,1,3,2,0:T(4,128)(2,1)} %copy.143) | data formatting | bytes 802816 | tf_op jit(solution)/shard_map/reshape;reshape | solution.py:59
  122.7 3.7 %copy.144 = bf16[2,4,49,16,32]{2,4,3,1,0:T(8,128)(2,1)} copy(bf16[2,4,49,16,32]{4,3,1,2,0:T(8,128)(2,1)} %reshape_reshape.7) | data formatting | bytes 802816 | tf_op jit(solution)/shard_map/reshape;reshape | solution.py:59
  126.4 4.5 %fusion.23 = bf16[2,4,49,16,32]{2,4,3,1,0:T(8,128)(2,1)} fusion(bf16[2,4,49,16,32]{2,4,3,1,0:T(8,128)(2,1)} %copy.144, f32[2,4,16,49,49]{3,4,2,1,0:T(8,128)} %copy-done.8, f32[2,4,16,49]{3,2,1,0:T(8,128)S(1)} %log_add_fusion), kind=kOutput, calls=%fused_computation.56 | convolution fusion | flops 20484352 | bytes 2057216 | tf_op jit(solution)/shard_map/bwhij,bwihd->bwjhd/dot_general | solution.py:416
  138.2 4.6 %copy.151 = bf16[2,4,49,16,32]{4,3,1,2,0:T(8,128)(2,1)} copy(bf16[2,4,49,16,32]{2,4,3,1,0:T(8,128)(2,1)} %fusion.23) | data formatting | bytes 802816 | tf_op jit(solution)/shard_map/bwhij,bwihd->bwjhd/transpose | solution.py:416
  145.4 4.6 %copy.146 = bf16[2,4,49,16,32]{4,3,1,2,0:T(8,128)(2,1)} copy(bf16[2,4,49,16,32]{2,4,3,1,0:T(8,128)(2,1)} %fusion.24) | data formatting | bytes 802816 | tf_op jit(solution)/shard_map/mul | solution.py:429
  150.0 3.7 %concatenate.52 = bf16[2,4,7,7,512]{4,1,3,2,0:T(4,128)(2,1)} reshape(bf16[2,4,49,16,32]{4,3,1,2,0:T(8,128)(2,1)} %copy.146) | data formatting | bytes 802816 | tf_op jit(solution)/shard_map/concatenate | solution.py:436
  153.7 4.6 %copy.148 = bf16[2,4,49,16,32]{4,3,1,2,0:T(8,128)(2,1)} copy(bf16[2,4,49,16,32]{2,4,3,1,0:T(8,128)(2,1)} %fusion.25) | data formatting | bytes 802816 | tf_op jit(solution)/shard_map/mul | solution.py:432
  158.2 3.3 %concatenate.53 = bf16[2,4,7,7,512]{4,1,3,2,0:T(4,128)(2,1)} reshape(bf16[2,4,49,16,32]{4,3,1,2,0:T(8,128)(2,1)} %copy.148) | data formatting | bytes 802816 | tf_op jit(solution)/shard_map/concatenate | solution.py:436
  168.9 2.7 convolution_convert_fusion.down
  180.5 5.2 %collective-permute-done.3 = bf16[2,3,28,1536]{3,0,2,1:T(2,128)(2,1)} collective-permute-done((bf16[2,3,28,1536]{3,0,2,1:T(2,128)(2,1)}, bf16[2,3,28,1536]{3,0,2,1:T(2,128)(2,1)}, u32[]{:S(2)}, u32[]{:S(2)}) %collective-permute-start.3) | collective-permute-done | bytes 516128 | tf_op jit(solution)/shard_map/ppermute | solution.py:29
  186.8 2.7 convert_reduce_fusion.2
  189.5 3.1 %reshape.238 = bf16[392,1536]{1,0:T(8,128)(2,1)} reshape(bf16[2,7,28,1536]{3,2,1,0:T(8,128)(2,1)} %get-tuple-element.141) | data formatting | bytes 2408448 | tf_op jit(solution)/shard_map/reshape | solution.py:446
  192.7 3.6 %fusion.16.qkv = bf16[512,1536]{1,0:T(8,128)(2,1)} fusion(bf16[2,7,28,1536]{3,2,1,0:T(8,128)(2,1)} %get-tuple-element.141, bf16[2,7,28,512]{3,0,2,1:T(2,128)(2,1)S(1)} %copy-done.41), kind=kOutput, calls=%fused_computation.36 | convolution fusion | flops 617349120 | bytes 3178496 | tf_op jit(solution)/shard_map/dot_general | solution.py:449
  201.6 63.2 %reduce_all.1 = (bf16[128,1536]{1,0:T(8,128)(2,1)S(1)}, bf16[128,512]{1,0:T(8,128)(2,1)S(1)}, bf16[128,2048]{1,0:T(8,128)(2,1)S(1)}, bf16[512,512]{1,0:T(8,128)(2,1)S(1)}, f32[72,128]{1,0:T(8,128)S(1)}) custom-call(bf16[512,1536]{1,0:T(8,128)(2,1)S(1)} %copy-done, bf16[512,512]{1,0:T(8,128)(2,1)S(1)} %convolution_convert_fusion.4.proj, ...), custom_call_target="tpu_custom_call" | custom-call | tf_op jit(solution)/shard_map/reduce_all/pallas_call | solution.py:238
  (253 shorter events, 91.7 us)
Async XLA Ops:
  7.2 25.4 %all-gather.4.cloned.1.call-start = ((), (), s32[]{:S(2)}) async-start(), calls=%async_computation | async-start | bytes 1966080 | tf_op jit(solution)/shard_map/all_gather | solution.py:329
  9.3 80.0 %all-gather.6.cloned.1.call-start = ((), (), s32[]{:S(2)}) async-start(), calls=%async_computation.1 | async-start | bytes 2621440 | tf_op jit(solution)/shard_map/all_gather | solution.py:331
  11.5 88.3 %all-gather.8.cloned.1.call-start = ((), (), s32[]{:S(2)}) async-start(), calls=%async_computation.2 | async-start | bytes 2621440 | tf_op jit(solution)/shard_map/all_gather | solution.py:332
  13.8 30.4 %copy-start.51 = (s32[2401]{0:T(1024)}, s32[2401]{0:T(1024)S(1)}, u32[]{:S(2)}) copy-start(s32[2401]{0:T(1024)S(1)} %eq.34) | copy-start | bytes 28816
  14.5 18.1 %copy-start.54 = (f32[392]{0:T(512)}, f32[392]{0:T(512)S(1)}, u32[]{:S(2)}) copy-start(f32[392]{0:T(512)S(1)} %div.117) | copy-start | bytes 4708
  14.8 21.1 %copy-start.56 = (f32[392]{0:T(512)}, f32[392]{0:T(512)S(1)}, u32[]{:S(2)}) copy-start(f32[392]{0:T(512)S(1)} %rsqrt.21) | copy-start | bytes 4708
  14.9 21.0 %copy-start.20 = (f32[392,512]{1,0:T(8,128)}, f32[392,512]{1,0:T(8,128)S(1)}, u32[]{:S(2)}) copy-start(f32[392,512]{1,0:T(8,128)S(1)} %reshape.223) | copy-start | bytes 2408452
  35.9 8.4 %copy-start.47 = (f32[16,169]{1,0:T(8,128)S(1)}, f32[16,169]{1,0:T(8,128)}, u32[]{:S(2)}) copy-start(f32[16,169]{1,0:T(8,128)} %param.41) | copy-start | bytes 32452
  35.9 9.6 %copy-start.58 = (s32[7,28]{1,0:T(8,128)S(1)}, s32[7,28]{1,0:T(8,128)}, u32[]{:S(2)}) copy-start(s32[7,28]{1,0:T(8,128)} %param.24) | copy-start | bytes 2356
  35.9 9.8 %copy-start.33 = (f32[128,512]{1,0:T(8,128)S(1)}, f32[128,512]{1,0:T(8,128)}, u32[]{:S(2)}) copy-start(f32[128,512]{1,0:T(8,128)} %param.29) | copy-start | bytes 786436
  39.5 16.5 %collective-permute-start = (bf16[2,3,28,1536]{3,0,2,1:T(2,128)(2,1)}, bf16[2,3,28,1536]{3,0,2,1:T(2,128)(2,1)}, u32[]{:S(2)}, u32[]{:S(2)}) collective-permute-start(bf16[2,3,28,1536]{3,0,2,1:T(2,128)(2,1)} %copy.128), channel_id=1, source_target_pairs={{4,0},{8,4},{12,8},{16,12},{20,16},{24,20},{28,24},{0,28},{5,1},{9... | collective-permute-start | bytes 1548296 | tf_op jit(solution)/shard_map/ppermute | solution.py:29
  67.3 5.9 %copy-start.40 = (bf16[128,512]{1,0:T(8,128)(2,1)S(1)}, bf16[128,512]{1,0:T(8,128)(2,1)}, u32[]{:S(2)}) copy-start(bf16[128,512]{1,0:T(8,128)(2,1)} %convert_element_type.105) | copy-start | bytes 393220
  72.4 15.4 %collective-permute-start.1 = (bf16[2,3,28,512]{3,0,2,1:T(2,128)(2,1)S(1)}, bf16[2,3,28,512]{3,0,2,1:T(2,128)(2,1)S(1)}, u32[]{:S(2)}, u32[]{:S(2)}) collective-permute-start(bf16[2,3,28,512]{3,0,2,1:T(2,128)(2,1)S(1)} %pad_maximum_fusion.5), channel_id=1, source_target_pairs={{28,0},{0,4},{4,8},{8,12},{12,16},{16,20},{20,24},{24,28},{29,1},{... | collective-permute-start | bytes 516104 | tf_op jit(solution)/shard_map/ppermute | solution.py:29
  88.5 11.3 %copy-start.26 = (bf16[392,512]{1,0:T(8,128)(2,1)}, bf16[392,512]{1,0:T(8,128)(2,1)S(1)}, u32[]{:S(2)}) copy-start(bf16[392,512]{1,0:T(8,128)(2,1)S(1)} %reshape.232) | copy-start | bytes 1204228
  89.1 22.2 %copy-start.19 = (f32[392,512]{1,0:T(8,128)}, f32[392,512]{1,0:T(8,128)S(1)}, u32[]{:S(2)}) copy-start(f32[392,512]{1,0:T(8,128)S(1)} %get-tuple-element.158) | copy-start | bytes 2408452
  89.4 10.4 %copy-start.27 = (f32[392,512]{1,0:T(8,128)S(1)}, f32[392,512]{1,0:T(8,128)}, u32[]{:S(2)}) copy-start(f32[392,512]{1,0:T(8,128)} %reshape.234) | copy-start | bytes 2408452
  105.7 5.6 %copy-start.60 = (f32[512]{0:T(512)S(1)}, f32[512]{0:T(512)}, u32[]{:S(2)}) copy-start(f32[512]{0:T(512)} %get-tuple-element.145) | copy-start | bytes 6148
  106.0 70.4 %copy-start.11 = (f32[392,512]{1,0:T(8,128)}, f32[392,512]{1,0:T(8,128)S(1)}, u32[]{:S(2)}) copy-start(f32[392,512]{1,0:T(8,128)S(1)} %get-tuple-element.139) | copy-start | bytes 2408452
  106.6 11.4 %collective-permute-start.2 = (bf16[2,3,28,512]{3,2,1,0:T(8,128)(2,1)S(1)}, bf16[2,3,28,512]{3,2,1,0:T(8,128)(2,1)S(1)}, u32[]{:S(2)}, u32[]{:S(2)}) collective-permute-start(bf16[2,3,28,512]{3,2,1,0:T(8,128)(2,1)S(1)} %slice.150), channel_id=1, source_target_pairs={{4,0},{8,4},{12,8},{16,12},{20,16},{24,20},{28,24},{0,28},{5,1},{9... | collective-permute-start | bytes 516104 | tf_op jit(solution)/shard_map/ppermute | solution.py:29
  165.1 6.5 %copy-start.30 = (bf16[2,7,3,1536]{3,2,1,0:T(4,128)(2,1)}, bf16[2,7,3,1536]{3,2,1,0:T(4,128)(2,1)S(1)}, u32[]{:S(2)}) copy-start(bf16[2,7,3,1536]{3,2,1,0:T(4,128)(2,1)S(1)} %copy.167) | copy-start | bytes 387076
  168.9 16.7 %collective-permute-start.3 = (bf16[2,3,28,1536]{3,0,2,1:T(2,128)(2,1)}, bf16[2,3,28,1536]{3,0,2,1:T(2,128)(2,1)}, u32[]{:S(2)}, u32[]{:S(2)}) collective-permute-start(bf16[2,3,28,1536]{3,0,2,1:T(2,128)(2,1)} %copy.155), channel_id=1, source_target_pairs={{28,0},{0,4},{4,8},{8,12},{12,16},{16,20},{20,24},{24,28},{29,1},{... | collective-permute-start | bytes 1548296 | tf_op jit(solution)/shard_map/ppermute | solution.py:29
  171.6 7.8 %copy-start.52 = (s32[2401]{0:T(1024)S(1)}, s32[2401]{0:T(1024)}, u32[]{:S(2)}) copy-start(s32[2401]{0:T(1024)} %copy-done.51) | copy-start | bytes 28816
  177.9 8.8 %copy-start.31 = (bf16[2,7,3,1536]{3,2,1,0:T(4,128)(2,1)S(1)}, bf16[2,7,3,1536]{3,2,1,0:T(4,128)(2,1)}, u32[]{:S(2)}) copy-start(bf16[2,7,3,1536]{3,2,1,0:T(4,128)(2,1)} %copy-done.30) | copy-start | bytes 387076
  186.8 5.9 %copy-start.41 = (bf16[2,7,28,512]{3,0,2,1:T(2,128)(2,1)S(1)}, bf16[2,7,28,512]{3,0,2,1:T(2,128)(2,1)}, u32[]{:S(2)}) copy-start(bf16[2,7,28,512]{3,0,2,1:T(2,128)(2,1)} %add_convert_fusion) | copy-start | bytes 1204228
  (49 other events, 166.3 us)
Sparse Core Ops, SparseCore 0:
  10.2 22.3 all-gather.3
  34.7 22.5 all-gather.5
  59.5 25.3 all-gather.7
